TPU v7x, 32 devices: a whole 2x2x4 slice. The times are simulated.
32 devices in a mesh: ta: 4 (over y, x), sa: 8 (over z, core).
Axes of the slice: x: 2, y: 2, z: 4, core: 2. Of those that a mesh axis runs over, the one named last changes fastest.
Arguments:
- perambulator: bfloat16 [2, 4, 8, 384, 384], P(None, None, 'sa', 'ta'), may hold values from -6 to 6
- meson_ops: bfloat16 [2, 8, 4, 384, 384], P(None, None, 'ta'), may hold values from -0.21875 to 0.21875
- diagram_lists: int32 [4, 64, 2], P('ta', 'sa'), may hold values from 0 to 63, as said below
Outputs:
- correlators: float32 [2, 4, 8, 384, 384], P(None, 'ta', 'sa')
Inputs may be any that keep to these rules, and one draw needn't show every extreme that they name: `diagram_lists`: every id lies in 0 to 63. Among the 16 ids of one owner's list, no spin pair (id // 8) occurs more than 2 times, and at least one spin pair occurs exactly 2 times; several may.
All inputs are finite; a program needn't handle non-finite values.
Results may differ from a plain program's by a relative error of at most 0.004.
Values may be sent and summed in bfloat16 or wider, within the bound.
A program may use at most 128 MiB of HBM per device.

v0:
```python
import jax
import jax.numpy as jnp
from jax import lax
from jax.sharding import PartitionSpec as P


def contract(first, second):
    return lax.dot_general(
        first, second, (((0, 2), (0, 1)), ((), ())), preferred_element_type=jnp.float32
    )


def body(perambulator, meson_ops, diagram_lists):
    regrouped = lax.all_to_all(perambulator, "ta", split_axis=1, concat_axis=3, tiled=True)
    operators = meson_ops[:, :, 0]
    ops_count = operators.shape[1]
    eig_count = operators.shape[2]
    pair_count = diagram_lists.shape[1]
    own_ids = diagram_lists[0].reshape(2 * pair_count)
    spin_ids = own_ids // ops_count
    op_ids = own_ids % ops_count
    all_spins = lax.all_gather(regrouped, "sa", axis=2, tiled=True)
    left_ops = jnp.take(operators, op_ids, axis=1)
    right_peram = jnp.take(all_spins[:, 0], spin_ids, axis=1)
    factor_real = jnp.einsum(
        "kab,kcb->kac", left_ops[0], right_peram[0], preferred_element_type=jnp.float32
    ) - jnp.einsum("kab,kcb->kac", left_ops[1], right_peram[1], preferred_element_type=jnp.float32)
    factor_imag = jnp.einsum(
        "kab,kcb->kac", left_ops[0], right_peram[1], preferred_element_type=jnp.float32
    ) + jnp.einsum("kab,kcb->kac", left_ops[1], right_peram[0], preferred_element_type=jnp.float32)
    factors = jnp.stack([factor_real, factor_imag], axis=1).astype(jnp.bfloat16)
    paired = factors.reshape(pair_count, 2, 2, eig_count, eig_count)
    left_real = paired[:, 0, 0]
    left_imag = paired[:, 0, 1]
    right_real = paired[:, 1, 0]
    right_imag = paired[:, 1, 1]
    real_sum = contract(left_real, right_real) - contract(left_imag, right_imag)
    imag_sum = contract(left_real, right_imag) + contract(left_imag, right_real)
    normalizer = 1.0 / jnp.sqrt(jnp.float32(2 * eig_count * pair_count))
    return (jnp.stack([real_sum, imag_sum]) * normalizer)[:, None, None]


def solution(mesh):
    in_specs = (
        P(None, None, "sa", "ta", None),
        P(None, None, "ta", None, None),
        P("ta", "sa", None),
    )
    out_specs = P(None, "ta", "sa", None, None)
    return jax.shard_map(body, mesh=mesh, in_specs=in_specs, out_specs=out_specs, check_vma=False)
```

profile of v0, /device:TPU:0, one launch (start us, length us, event | category | flops | bytes accessed | tf_op | source)
XLA Modules:
  0.0 148.7 jit_solution(15078473945187081545)
XLA Ops:
  6.5 0.0 all-gather.2.cloned.1.call-start
  6.5 1.1 copy.18
  7.7 14.4 %all_to_all.12 = bf16[2,4,1,96,384]{4,3,2,0,1:T(8,128)(2,1)S(1)} all-to-all(bf16[2,4,1,96,384]{4,3,2,0,1:T(8,128)(2,1)S(1)} %copy.18), channel_id=1, replica_groups=mesh['ta'=4,'sa'=8] {'ta'}, dimensions={1} | all-to-all | bytes 1179648 | tf_op jit(solution)/shard_map/all_to_all | solution.py:14
  22.0 0.9 copy.19
  22.9 0.0 all-gather.2.cloned.1.call-update
  22.9 0.8 copy.16
  23.7 0.1 reshape_squeeze.3
  23.8 8.0 %gather_fusion = bf16[16,2,384,384]{3,2,1,0:T(8,128)(2,1)} fusion(bf16[2,8,384,384]{3,2,1,0:T(8,128)(2,1)} %bitcast.109, s32[1024]{0:T(1024)S(1)} %pad_clamp_fusion.1), kind=kCustom, calls=%fused_computation.clone | custom fusion | bytes 18874432 | tf_op jit(solution)/shard_map/jit(_take)/gather | solution.py:23
  31.8 8.4 %fusion.1 = bf16[2,16,384,384]{3,2,1,0:T(8,128)(2,1)} fusion(bf16[16,2,384,384]{3,2,1,0:T(8,128)(2,1)} %gather_fusion, pred[16]{0:T(512)(128)(4,1)S(1)} %get-tuple-element.10), kind=kLoop, calls=%fused_computation.5 | loop fusion | flops 4718592 | bytes 18874384 | tf_op jit(solution)/shard_map/jit(_take)/select_n | solution.py:23
  40.3 34.0 %all-gather.2.cloned.1.call-done = bf16[2,1,8,384,384]{4,3,2,0,1:T(8,128)(2,1)} async-done(((bf16[2,1,1,384,384]{4,3,2,0,1:T(8,128)(2,1)}), bf16[2,1,8,384,384]{4,3,2,0,1:T(8,128)(2,1)}) %all-gather.2.cloned.1.call-update) | async-done | bytes 4718608 | tf_op jit(solution)/shard_map/all_gather | solution.py:22
  74.3 8.0 %gather_fusion.1 = bf16[16,2,384,384]{3,2,1,0:T(8,128)(2,1)} fusion(bf16[2,8,384,384]{3,2,1,0:T(8,128)(2,1)} %bitcast.110, s32[1024]{0:T(1024)S(1)} %pad_clamp_fusion), kind=kCustom, calls=%fused_computation.1.clone | custom fusion | bytes 18874432 | tf_op jit(solution)/shard_map/jit(_take)/gather | solution.py:24
  82.3 8.5 %fusion = bf16[2,16,384,384]{3,2,1,0:T(8,128)(2,1)} fusion(bf16[16,2,384,384]{3,2,1,0:T(8,128)(2,1)} %gather_fusion.1, pred[16]{0:T(512)(128)(4,1)S(1)} %get-tuple-element.6), kind=kLoop, calls=%fused_computation.3 | loop fusion | flops 4718592 | bytes 18874384 | tf_op jit(solution)/shard_map/jit(_take)/select_n | solution.py:24
  90.8 0.0 copy-start
  90.8 10.8 %fusion.3 = f32[16,384,384]{2,1,0:T(8,128)} fusion(bf16[2,16,384,384]{3,2,1,0:T(8,128)(2,1)} %fusion.1, bf16[2,16,384,384]{3,2,1,0:T(8,128)(2,1)} %fusion), kind=kOutput, calls=%fused_computation.13 | convolution fusion | flops 1811939328 | bytes 18874368 | tf_op jit(solution)/shard_map/kab,kcb->kac/dot_general | solution.py:25
  101.6 0.0 copy-done
  101.6 9.3 %fusion.2 = f32[16,384,384]{2,1,0:T(8,128)} fusion(bf16[2,16,384,384]{3,2,1,0:T(8,128)(2,1)} %fusion.1, bf16[2,16,384,384]{3,2,1,0:T(8,128)(2,1)S(1)} %copy-done), kind=kOutput, calls=%fused_computation.12 | convolution fusion | flops 1811939328 | bytes 18874368 | tf_op jit(solution)/shard_map/kab,kcb->kac/dot_general | solution.py:28
  110.9 9.7 %subtract_convert_fusion = bf16[16,384,384]{2,1,0:T(8,128)(2,1)S(1)} fusion(f32[16,384,384]{2,1,0:T(8,128)} %fusion.3, bf16[2,16,384,384]{3,2,1,0:T(8,128)(2,1)} %fusion, bf16[2,16,384,384]{3,2,1,0:T(8,128)(2,1)} %fusion.1), kind=kOutput, calls=%fused_computation.7 | convolution fusion | flops 1816657920 | bytes 23592960 | tf_op jit(solution)/shard_map/kab,kcb->kac/dot_general | solution.py:27
  120.6 12.1 %add_convert_fusion = bf16[16,384,384]{2,1,0:T(8,128)(2,1)} fusion(f32[16,384,384]{2,1,0:T(8,128)} %fusion.2, bf16[2,16,384,384]{3,2,1,0:T(8,128)(2,1)} %fusion, bf16[2,16,384,384]{3,2,1,0:T(8,128)(2,1)} %fusion.1), kind=kOutput, calls=%fused_computation.6 | convolution fusion | flops 1816657920 | bytes 23592960 | tf_op jit(solution)/shard_map/kab,kcb->kac/dot_general | solution.py:30
  132.6 0.0 copy-start.1
  132.6 3.9 %fusion.10 = f32[384,384]{1,0:T(8,128)S(1)} fusion(bf16[8,2,1,384,384]{4,3,1,0,2:T(8,128)(2,1)} %bitcast.114), kind=kOutput, calls=%fused_computation.24 | convolution fusion | flops 905969664 | bytes 5308416 | tf_op jit(solution)/shard_map/dot_general | solution.py:8
  136.5 0.0 copy-done.1
  136.5 1.4 fusion.11
  137.9 1.4 fusion.15
  139.4 1.4 fusion.17
  140.7 1.1 maximum_multiply_fusion
  (3 shorter events, 0.0 us)
Async XLA Ops:
  6.5 67.8 %all-gather.2.cloned.1.call-start = ((), (), s32[]{:S(2)}) async-start(), calls=%async_computation.1 | async-start | bytes 5308416 | tf_op jit(solution)/shard_map/all_gather | solution.py:22
  90.8 10.8 %copy-start = (bf16[2,16,384,384]{3,2,1,0:T(8,128)(2,1)S(1)}, bf16[2,16,384,384]{3,2,1,0:T(8,128)(2,1)}, u32[]{:S(2)}) copy-start(bf16[2,16,384,384]{3,2,1,0:T(8,128)(2,1)} %fusion) | copy-start | bytes 28311556
  132.6 3.9 %copy-start.1 = (bf16[16,384,384]{2,1,0:T(8,128)(2,1)S(1)}, bf16[16,384,384]{2,1,0:T(8,128)(2,1)}, u32[]{:S(2)}) copy-start(bf16[16,384,384]{2,1,0:T(8,128)(2,1)} %add_convert_fusion) | copy-start | bytes 14155780
Sparse Core Ops, SparseCore 0:
  23.0 51.2 all-gather.1
where the time goes:
time: 149 us
  matrix products  49.9 us (33%)
  waiting for transfers between devices  34.1 us (23%)
  local copies, waits for them, and re-layouts  18.9 us (13%)
  other arithmetic  18 us (12%)
  blocking collectives  14.4 us (10%)
  between operations  13.5 us (9%)
    all_gather x1, waiting for transfers between devices, body(): all_spins = lax.all_gather(regrouped, 'sa', axis=2, tiled=True)  34 us
    all_to_all x1, blocking collectives, body(): lax.all_to_all(perambulator, 'ta', split_axis=1, concat_axis=3, tiled=True)  14.4 us
    dot_general x1, matrix products, body(): jnp.einsum('kab,kcb->kac', left_ops[1], right_peram[0], preferred_element...  12.1 us
    dot_general x1, matrix products, body(): jnp.einsum('kab,kcb->kac', left_ops[0], right_peram[0], preferred_element...  10.8 us
    dot_general x1, matrix products, body(): jnp.einsum('kab,kcb->kac', left_ops[1], right_peram[1], preferred_element...  9.68 us
    dot_general x1, matrix products, body(): jnp.einsum('kab,kcb->kac', left_ops[0], right_peram[1], preferred_element...  9.28 us
    select_n x1, other arithmetic, body(): right_peram = jnp.take(all_spins[:, 0], spin_ids, axis=1)  8.48 us
    select_n x1, other arithmetic, body(): left_ops = jnp.take(operators, op_ids, axis=1)  8.4 us
  transfers between devices with their start and end apart: 1, of which 1 were waited for; matrix products, arithmetic and copies ran while one was open for 12% of the time, Pallas kernels for 0%

commit v1 on v0

v1 whole, which is shorter than its diff:
```python
import functools

import jax
import jax.numpy as jnp
from jax import lax
from jax.experimental import pallas as pl
from jax.experimental.pallas import tpu as pltpu
from jax.sharding import PartitionSpec as P

CORES = 2
CAP = 2
MESH = pl.DeviceIdType.MESH


def kernel(
    ta, sa, op_table, pair_slots, peram, ops, out, held, ops_here, factors, total,
    send_sem, recv_sem, local_sem,
):
    chips = sa // CORES
    half = chips // 2
    a = lax.axis_index("ta")
    me = lax.axis_index("sa")
    z, core = me // CORES, lax.rem(me, CORES)
    eig = ops.shape[-1]

    def spin_at(offset, parity):
        return lax.rem(z + offset + chips, chips) * CORES + parity

    up = (a, spin_at(1, core))
    down = (a, spin_at(-1, core))
    sibling = (a, z * CORES + 1 - core)
    plane = [(lax.rem(a + j, ta), me) for j in range(1, ta)]

    load_ops = pltpu.make_async_copy(ops.at[:, :, 0], ops_here, local_sem.at[0])
    load_ops.start()
    load_own = pltpu.make_async_copy(peram.at[:, a, 0], held.at[me, 0], local_sem.at[1])
    load_own.start()

    barrier = pltpu.get_barrier_semaphore()
    peers = [*plane, up, down, sibling]
    for peer in peers:
        pl.semaphore_signal(barrier, inc=1, device_id=peer, device_id_type=MESH)
    pl.semaphore_wait(barrier, len(peers))

    sent = []

    def send(src, spin, slot, peer):
        copy = pltpu.make_async_remote_copy(
            src_ref=src,
            dst_ref=held.at[spin, slot],
            send_sem=send_sem.at[len(sent)],
            recv_sem=recv_sem.at[spin, slot],
            device_id=peer,
            device_id_type=MESH,
        )
        copy.start()
        sent.append(copy)

    def arrived(spin, slot):
        pltpu.make_async_remote_copy(
            src_ref=held.at[spin, slot],
            dst_ref=held.at[spin, slot],
            send_sem=send_sem.at[0],
            recv_sem=recv_sem.at[spin, slot],
            device_id=sibling,
            device_id_type=MESH,
        ).wait_recv()

    def hops_up(i):
        return half if i < ta // 2 else chips - 1 - half

    def hops_down(i):
        return chips - 1 - hops_up(i)

    def factor(spin):
        at = [lax.rem(q - a + ta, ta) for q in range(ta)]
        real = jnp.concatenate([held[spin, i, 0] for i in at], axis=0)
        imag = jnp.concatenate([held[spin, i, 1] for i in at], axis=0)
        right = jnp.concatenate(
            [jnp.concatenate([real, -imag], axis=1), jnp.concatenate([imag, real], axis=1)], axis=0
        )
        lefts = []
        for c in range(CAP):
            op = op_table[spin * CAP + c]
            lefts.append(jnp.concatenate([ops_here[0, op], ops_here[1, op]], axis=1))
        both = lax.dot_general(
            jnp.concatenate(lefts, axis=0), right, (((1,), (1,)), ((), ())),
            preferred_element_type=jnp.float32,
        )
        for c in range(CAP):
            factors[spin * CAP + c] = both[c * eig:(c + 1) * eig].astype(jnp.bfloat16)

    own = peram.at[:, a, 0]
    for peer in (up, down, sibling):
        send(own, me, 0, peer)
    for j in range(1, ta):
        send(peram.at[:, plane[j - 1][0], 0], me, ta - j, plane[j - 1])
    for i in range(ta - 1, 0, -1):
        arrived(me, i)
        for peer in (up, down, sibling):
            send(held.at[me, i], me, i, peer)

    load_ops.wait()
    load_own.wait()
    other = z * CORES + 1 - core
    for i in range(ta):
        arrived(other, i)

    def own_chip(n, carry):
        factor(z * CORES + n)
        return carry

    lax.fori_loop(0, CORES, own_chip, 0)

    for h in range(1, half + 1):
        below, above = spin_at(-h, core), spin_at(h, core)
        order = [0, *range(ta - 1, 0, -1)]
        for i in order:
            if hops_up(i) >= h:
                arrived(below, i)
                if hops_up(i) > h:
                    send(held.at[below, i], below, i, up)
                send(held.at[below, i], below, i, sibling)
            if hops_down(i) >= h:
                arrived(above, i)
                if hops_down(i) > h:
                    send(held.at[above, i], above, i, down)
                send(held.at[above, i], above, i, sibling)
        count = 2 if 2 * h < chips else 1

        def ready(n, carry):
            factor(spin_at(jnp.where(n == 0, -h, h), core))
            return carry

        lax.fori_loop(0, count, ready, 0)
        for offset in (-h, h)[:count]:
            for i in range(ta):
                arrived(spin_at(offset, 1 - core), i)

        def siblings(n, carry):
            factor(spin_at(jnp.where(n == 0, -h, h), 1 - core))
            return carry

        lax.fori_loop(0, count, siblings, 0)

    total[...] = jnp.zeros_like(total)

    def pair(p, carry):
        left = factors[pair_slots[2 * p]]
        second = factors[pair_slots[2 * p + 1]]
        real, imag = second[:, :eig], second[:, eig:]
        right = jnp.concatenate([second, jnp.concatenate([-imag, real], axis=1)], axis=0)
        total[...] += jnp.dot(left, right, preferred_element_type=jnp.float32)
        return carry

    pairs = pair_slots.shape[0] // 2
    lax.fori_loop(0, pairs, pair, 0)
    normalizer = 1.0 / jnp.sqrt(jnp.float32(2 * eig * pairs))
    out[0] = total[:, :eig] * normalizer
    out[1] = total[:, eig:] * normalizer
    for copy in sent:
        copy.wait_send()


def body(ta, sa, perambulator, meson_ops, diagram_lists):
    ops_count, eig = meson_ops.shape[1], meson_ops.shape[-1]
    rows = perambulator.shape[3]
    ids = diagram_lists[0].reshape(-1)
    spins = ids // ops_count
    ahead = jnp.arange(ids.shape[0])[:, None] > jnp.arange(ids.shape[0])[None, :]
    rank = jnp.sum((spins[:, None] == spins[None, :]) & ahead, axis=1, dtype=jnp.int32)
    slots = spins * CAP + rank
    here = slots[None, :] == jnp.arange(sa * CAP)[:, None]
    op_table = jnp.sum(jnp.where(here, (ids % ops_count)[None, :], 0), axis=1, dtype=jnp.int32)
    chips = sa // CORES
    sends = (ta - 1) + ta * (chips - 1 + chips)
    flops = 2 * (2 * eig) ** 2 * eig * (sa * CAP + ids.shape[0] // 2)
    result = pl.pallas_call(
        functools.partial(kernel, ta, sa),
        out_shape=jax.ShapeDtypeStruct((2, eig, eig), jnp.float32),
        in_specs=[
            pl.BlockSpec(memory_space=pltpu.SMEM),
            pl.BlockSpec(memory_space=pltpu.SMEM),
            pl.BlockSpec(memory_space=pl.ANY),
            pl.BlockSpec(memory_space=pl.ANY),
        ],
        out_specs=pl.BlockSpec(memory_space=pltpu.VMEM),
        scratch_shapes=[
            pltpu.VMEM((sa, ta, 2, rows, eig), jnp.bfloat16),
            pltpu.VMEM((2, ops_count, eig, eig), jnp.bfloat16),
            pltpu.VMEM((sa * CAP, eig, 2 * eig), jnp.bfloat16),
            pltpu.VMEM((eig, 2 * eig), jnp.float32),
            pltpu.SemaphoreType.DMA((sends,)),
            pltpu.SemaphoreType.DMA((sa, ta)),
            pltpu.SemaphoreType.DMA((2,)),
        ],
        compiler_params=pltpu.CompilerParams(
            collective_id=0, has_side_effects=True, vmem_limit_bytes=56 * 2**20
        ),
        cost_estimate=pl.CostEstimate(
            flops=flops, bytes_accessed=4 * meson_ops.size, transcendentals=0
        ),
    )(op_table, slots, perambulator, meson_ops)
    return result[:, None, None]


def solution(mesh):
    in_specs = (
        P(None, None, "sa", "ta", None),
        P(None, None, "ta", None, None),
        P("ta", "sa", None),
    )
    out_specs = P(None, "ta", "sa", None, None)
    return jax.shard_map(
        functools.partial(body, mesh.shape["ta"], mesh.shape["sa"]),
        mesh=mesh, in_specs=in_specs, out_specs=out_specs, check_vma=False,
    )
```

time: 149 us -> 60.8 us (0.41)
  Pallas kernels: 0 us -> 56.5 us
  matrix products: 49.9 us -> 0 us
  waiting for transfers between devices: 34.1 us -> 0 us
  other arithmetic: 18 us -> 0.83 us
  local copies, waits for them, and re-layouts: 18.9 us -> 3.2 us
  blocking collectives: 14.4 us -> 0 us
  between operations: 13.5 us -> 0.02 us
    pallas_call x0 -> x1, Pallas kernels: none -> 56.5 us  [body(): pl.pallas_call(functools.partial(kernel, ta, sa), out_shape=jax.ShapeDtyp...]
    dot_general x8 -> x0, matrix products: 49.9 us -> none  [the longest x1 12.1 us: body(): jnp.einsum('kab,kcb->kac', left_ops[1], right_peram[0], preferred_element...]
    all_gather x1 -> x0, waiting for transfers between devices: 34 us -> none  [body(): all_spins = lax.all_gather(regrouped, 'sa', axis=2, tiled=True)]
    select_n x2 -> x1, other arithmetic: 16.9 us -> 0.01 us  [body(): spins = ids // ops_count]
    gather x2 -> x0, local copies, waits for them, and re-layouts: 16.1 us -> none  [the longest x1 8.04 us: body(): left_ops = jnp.take(operators, op_ids, axis=1)]
    all_to_all x1 -> x0, blocking collectives: 14.4 us -> none  [body(): lax.all_to_all(perambulator, 'ta', split_axis=1, concat_axis=3, tiled=True)]
    unnamed x6 -> x4, local copies, waits for them, and re-layouts: 1.89 us -> 3.12 us
  transfers between devices with their start and end apart: 1 -> 0, of which waited for: 1 -> 0; matrix products, arithmetic and copies ran while one was open for 12% -> 0% of each run, Pallas kernels for 0% -> 0%
where the time goes in v1:
time: 60.8 us; the launch traced here: 60.6 us
  Pallas kernels  56.5 us (93%)
  local copies, waits for them, and re-layouts  3.2 us (5%)
  other arithmetic  0.83 us (1%)
    pallas_call x1, Pallas kernels, body(): pl.pallas_call(functools.partial(kernel, ta, sa), out_shape=jax.ShapeDtyp...  56.5 us
    unnamed x4, local copies, waits for them, and re-layouts  3.12 us

profile of v1, /device:TPU:0, one launch (start us, length us, event | category | flops | bytes accessed | tf_op | source)
XLA Modules:
  0.0 60.6 jit_solution(6515077034326917101)
XLA Ops:
  0.0 0.8 %copy.8 = s32[1,8,2]{2,1,0:T(8,128)S(1)} copy(s32[1,8,2]{1,2,0:T(2,128)} %param.5) | data formatting | bytes 128 | tf_op args[2]
  0.8 0.1 reshape_squeeze.3
  0.8 0.2 convert_reduce_fusion
  1.0 0.0 copy-start
  1.1 0.6 %select_reduce_fusion.op_table = s32[16]{0:T(128)} fusion(s32[16]{0:T(128)S(1)} %get-tuple-element.6, s32[16]{0:T(128)S(1)} %multiply_add_fusion.pair_slots), kind=kLoop, calls=%fused_computation | loop fusion | flops 752 | bytes 192 | tf_op jit(solution)/shard_map/reduce_sum | solution.py:174
  1.7 0.0 copy-done
  1.7 56.5 %shard_map.37 = f32[2,384,384]{2,1,0:T(8,128)} custom-call(s32[16]{0:T(128)} %select_reduce_fusion.op_table, s32[16]{0:T(128)} %copy-done, bf16[2,4,1,96,384]{4,3,2,1,0:T(8,128)(2,1)} %peram.1, bf16[2,8,1,384,384]{4,3,2,1,0:T(8,128)(2,1)} %ops.1), custom_call_target="tpu_custom_call" | custom-call | flops 10871635968 | bytes 9437184 | tf_op jit(solution)/shard_map/pallas_call | solution.py:178
  58.2 2.4 %copy.11 = f32[2,1,1,384,384]{4,3,2,1,0:T(8,128)} copy(f32[2,1,1,384,384]{4,3,2,1,0:T(8,128)} %bitcast.3) | data formatting | bytes 2359296
  (2 shorter events, 0.0 us)
Async XLA Ops:
  1.0 0.6 %copy-start = (s32[16]{0:T(128)}, s32[16]{0:T(128)S(1)}, u32[]{:S(2)}) copy-start(s32[16]{0:T(128)S(1)} %multiply_add_fusion.pair_slots) | copy-start | bytes 196

commit v2 on v1

--- a/solution.py
+++ b/solution.py
@@ -13,7 +13,7 @@
 
 
 def kernel(
-    ta, sa, op_table, pair_slots, peram, ops, out, held, ops_here, factors, total,
+    ta, sa, op_table, pair_slots, peram, ops, out, held, ops_here, factors,
     send_sem, recv_sem, local_sem,
 ):
     chips = sa // CORES
@@ -100,6 +100,7 @@
         for peer in (up, down, sibling):
             send(held.at[me, i], me, i, peer)
 
+    out[...] = jnp.zeros_like(out)
     load_ops.wait()
     load_own.wait()
     other = z * CORES + 1 - core
@@ -143,21 +144,18 @@
 
         lax.fori_loop(0, count, siblings, 0)
 
-    total[...] = jnp.zeros_like(total)
-
     def pair(p, carry):
         left = factors[pair_slots[2 * p]]
         second = factors[pair_slots[2 * p + 1]]
         real, imag = second[:, :eig], second[:, eig:]
         right = jnp.concatenate([second, jnp.concatenate([-imag, real], axis=1)], axis=0)
-        total[...] += jnp.dot(left, right, preferred_element_type=jnp.float32)
+        both = jnp.dot(left, right, preferred_element_type=jnp.float32)
+        out[0] += both[:, :eig]
+        out[1] += both[:, eig:]
         return carry
 
     pairs = pair_slots.shape[0] // 2
-    lax.fori_loop(0, pairs, pair, 0)
-    normalizer = 1.0 / jnp.sqrt(jnp.float32(2 * eig * pairs))
-    out[0] = total[:, :eig] * normalizer
-    out[1] = total[:, eig:] * normalizer
+    lax.fori_loop(0, pairs, pair, 0, unroll=2)
     for copy in sent:
         copy.wait_send()
 
@@ -189,7 +187,6 @@
             pltpu.VMEM((sa, ta, 2, rows, eig), jnp.bfloat16),
             pltpu.VMEM((2, ops_count, eig, eig), jnp.bfloat16),
             pltpu.VMEM((sa * CAP, eig, 2 * eig), jnp.bfloat16),
-            pltpu.VMEM((eig, 2 * eig), jnp.float32),
             pltpu.SemaphoreType.DMA((sends,)),
             pltpu.SemaphoreType.DMA((sa, ta)),
             pltpu.SemaphoreType.DMA((2,)),
@@ -201,7 +198,8 @@
             flops=flops, bytes_accessed=4 * meson_ops.size, transcendentals=0
         ),
     )(op_table, slots, perambulator, meson_ops)
-    return result[:, None, None]
+    normalizer = 1.0 / jnp.sqrt(jnp.float32(ids.shape[0] * eig))
+    return (result * normalizer)[:, None, None]
 
 
 def solution(mesh):

time: 60.8 us -> 59.9 us (0.985)
  other arithmetic: 0.83 us -> 3.22 us
  local copies, waits for them, and re-layouts: 3.2 us -> 0.84 us
  Pallas kernels: 56.5 us -> 55.7 us
    broadcast_in_dim x0 -> x1, other arithmetic: none -> 2.39 us  [body(): return (result * normalizer)[:, None, None]]
    unnamed x4 -> x3, local copies, waits for them, and re-layouts: 3.12 us -> 0.76 us
    pallas_call x1, Pallas kernels: 56.5 us -> 55.7 us  [body(): pl.pallas_call(functools.partial(kernel, ta, sa), out_shape=jax.ShapeDtyp...]
where the time goes in v2:
time: 59.9 us; the launch traced here: 59.8 us
  Pallas kernels  55.7 us (93%)
  other arithmetic  3.22 us (5%)
  local copies, waits for them, and re-layouts  0.84 us (1%)
    pallas_call x1, Pallas kernels, body(): pl.pallas_call(functools.partial(kernel, ta, sa), out_shape=jax.ShapeDtyp...  55.7 us
    broadcast_in_dim x1, other arithmetic, body(): return (result * normalizer)[:, None, None]  2.39 us

profile of v2, /device:TPU:0, one launch (start us, length us, event | category | flops | bytes accessed | tf_op | source)
XLA Modules:
  0.0 59.8 jit_solution(17330532488388175591)
XLA Ops:
  0.0 0.8 %copy.8 = s32[1,8,2]{2,1,0:T(8,128)S(1)} copy(s32[1,8,2]{1,2,0:T(2,128)} %param.5) | data formatting | bytes 128 | tf_op args[2]
  0.8 0.1 reshape_squeeze.3
  0.8 0.2 convert_reduce_fusion
  1.0 0.0 copy-start
  1.1 0.6 %select_reduce_fusion.op_table = s32[16]{0:T(128)} fusion(s32[16]{0:T(128)S(1)} %get-tuple-element.6, s32[16]{0:T(128)S(1)} %multiply_add_fusion.pair_slots), kind=kLoop, calls=%fused_computation.1 | loop fusion | flops 752 | bytes 192 | tf_op jit(solution)/shard_map/reduce_sum | solution.py:172
  1.7 0.0 copy-done
  1.7 55.7 %shard_map.37 = f32[2,384,384]{2,1,0:T(8,128)} custom-call(s32[16]{0:T(128)} %select_reduce_fusion.op_table, s32[16]{0:T(128)} %copy-done, bf16[2,4,1,96,384]{4,3,2,1,0:T(8,128)(2,1)} %peram.1, bf16[2,8,1,384,384]{4,3,2,1,0:T(8,128)(2,1)} %ops.1), custom_call_target="tpu_custom_call" | custom-call | flops 10871635968 | bytes 9437184 | tf_op jit(solution)/shard_map/pallas_call | solution.py:176
  57.4 2.4 %multiply_bitcast_fusion = f32[2,1,1,384,384]{4,3,2,1,0:T(8,128)} fusion(f32[2,384,384]{2,1,0:T(8,128)} %shard_map.37), kind=kLoop, calls=%fused_computation | loop fusion | flops 294912 | bytes 2359296 | tf_op jit(solution)/shard_map/broadcast_in_dim | solution.py:202
  (2 shorter events, 0.0 us)
Async XLA Ops:
  1.0 0.6 %copy-start = (s32[16]{0:T(128)}, s32[16]{0:T(128)S(1)}, u32[]{:S(2)}) copy-start(s32[16]{0:T(128)S(1)} %multiply_add_fusion.pair_slots) | copy-start | bytes 196
